TPU v7x, 128 devices: a whole 4x4x4 slice. The times are simulated.
128 devices in a mesh: dp: 16 (over x, y), expert: 8 (over z, core).
Axes of the slice: x: 4, y: 4, z: 4, core: 2. Of those that a mesh axis runs over, the one named last changes fastest.
Arguments:
- hidden: bfloat16 [16384, 2, 7168], P(('dp', 'expert')), may hold values from -6 to 6
- grad_out: bfloat16 [16384, 2048], P(('dp', 'expert')), may hold values from -6 to 6
- gate_weights: float32 [16384, 2], P(('dp', 'expert')), may hold values from 0.1 to 1
- routes: int32 [16384, 2], P(('dp', 'expert')), may hold values from 0 to 7, all different within a row; in each aligned block of 128 rows (0 to 127, 128 to 255, ...) at most 48 rows name the same one
- example_ids: int32 [16384], P(('dp', 'expert')), may hold values from 0 to 127, as said below
Outputs:
- update: bfloat16 [8, 7168, 2048], P('expert', 'dp')
- norm_ratio: float32 [128], P('dp')
Inputs may be any that keep to these rules, and one draw needn't show every extreme that they name: `routes`: among the 128 tokens of one device no expert is named by more than 48 tokens, and some device reaches 48 for some expert. `example_ids`: ids never fall along the tokens; tokens i * 1024 to (i + 1) * 1024 - 1 hold exactly the examples i * 8 to (i + 1) * 8 - 1, each with one or more tokens.
All inputs are finite; a program needn't handle non-finite values.
Results may differ from a plain program's by a relative error of at most 0.019.
Values may be sent and summed in bfloat16 or wider, within the bound.
A program may use at most 128 MiB of HBM per device.

v0:
```python
import math
import jax
import jax.numpy as jnp
from jax import lax
from jax.sharding import PartitionSpec as P

EX_BLK = 8


def body(hidden, grad_out, gate_weights, routes, example_ids):
    experts = lax.axis_size("expert")
    replicas = lax.axis_size("dp")
    replica = lax.axis_index("dp")
    tokens_here = hidden.shape[0]
    hidden_width = hidden.shape[2]
    out_width = grad_out.shape[1]
    capacity = 3 * tokens_here // experts
    row_count = experts * capacity
    examples = EX_BLK * replicas
    threshold = math.sqrt(hidden_width * out_width * tokens_here * (0.43 + 0.01 * tokens_here))
    grad_rows = (gate_weights[:, :, None] * grad_out[:, None, :].astype(jnp.float32)).astype(
        jnp.bfloat16
    )
    route_flat = routes.reshape(-1)
    chosen = (route_flat[:, None] == jnp.arange(experts, dtype=jnp.int32)[None, :]).astype(
        jnp.int32
    )
    position = jnp.sum((jnp.cumsum(chosen, axis=0) - 1) * chosen, axis=1)
    destin = route_flat * capacity + position
    hidden_sent = (
        jnp.zeros((experts * capacity, hidden_width), jnp.bfloat16)
        .at[destin]
        .set(hidden.reshape(-1, hidden_width))
    )
    grads_sent = (
        jnp.zeros((experts * capacity, out_width), jnp.bfloat16)
        .at[destin]
        .set(grad_rows.reshape(-1, out_width))
    )
    owner_sent = (
        jnp.full((experts * capacity,), -1, jnp.int32).at[destin].set(jnp.repeat(example_ids, 2))
    )
    hidden_in, grads_in, owner_in = (
        lax.all_to_all(
            hidden_sent.reshape(experts, capacity, hidden_width),
            "expert",
            split_axis=0,
            concat_axis=0,
            tiled=True,
        ),
        lax.all_to_all(
            grads_sent.reshape(experts, capacity, out_width),
            "expert",
            split_axis=0,
            concat_axis=0,
            tiled=True,
        ),
        lax.all_to_all(
            owner_sent.reshape(experts, capacity), "expert", split_axis=0, concat_axis=0, tiled=True
        ),
    )
    hidden_in = hidden_in.reshape(row_count, hidden_width)
    grads_in = grads_in.reshape(row_count, out_width)
    owner_in = owner_in.reshape(row_count)
    first_example = replica * EX_BLK
    belongs = (
        owner_in[:, None] == first_example + jnp.arange(EX_BLK, dtype=jnp.int32)[None, :]
    ).astype(jnp.float32)
    hidden_gram = jnp.dot(hidden_in, hidden_in.T, preferred_element_type=jnp.float32)
    grad_gram = jnp.dot(grads_in, grads_in.T, preferred_element_type=jnp.float32)
    matched = (owner_in[:, None] == owner_in[None, :]).astype(jnp.float32)
    row_sums = jnp.sum(hidden_gram * grad_gram * matched, axis=1)
    square_part = jnp.sum(row_sums[:, None] * belongs, axis=0)
    squares = lax.psum(square_part, "expert")
    norm_values = jnp.sqrt(squares)
    factors = jnp.minimum(1.0, threshold / norm_values)
    row_factors = jnp.sum(belongs * factors[None, :], axis=1)
    clipped = (row_factors[:, None] * grads_in.astype(jnp.float32)).astype(jnp.bfloat16)
    shard_width = hidden_width // replicas
    reduced = lax.psum_scatter(
        lax.dot_general(
            hidden_in, clipped, (((0,), (0,)), ((), ())), preferred_element_type=jnp.float32
        ).astype(jnp.bfloat16),
        "dp",
        scatter_dimension=0,
        tiled=True,
    ).astype(jnp.float32)
    update = (reduced / examples).astype(jnp.bfloat16).reshape(1, shard_width, out_width)
    return (update, norm_values / threshold)


def solution(mesh):
    return jax.shard_map(
        body,
        mesh=mesh,
        in_specs=(
            P(("dp", "expert"), None, None),
            P(("dp", "expert"), None),
            P(("dp", "expert"), None),
            P(("dp", "expert"), None),
            P(("dp", "expert")),
        ),
        out_specs=(P("expert", "dp", None), P("dp")),
        check_vma=False,
    )
```

profile of v0, /device:TPU:1, one launch (start us, length us, event | category | flops | bytes accessed | tf_op | source)
XLA Modules:
  0.0 352.0 jit_solution(234594148419169205)
XLA Ops:
  7.2 0.7 broadcast_multiply_fusion
  7.8 0.8 copy.12
  8.6 0.1 eq.57
  8.8 0.1 eq.53
  9.0 0.1 mul.75
  9.2 0.6 reduce-window.6
  9.8 0.2 slice_reduce_fusion
  10.0 0.7 broadcast_in_dim.10
  10.8 0.1 reshape.122
  11.0 1.4 scatter_custom_fusion.1
  12.4 0.7 all_to_all.13
  13.1 6.8 %all-to-all-start.1 = ((s32[8,1,48]{2,1,0:T(1,128)}), s32[8,1,48]{2,1,0:T(1,128)S(1)}, u32[]{:S(2)}, u32[]{:S(2)}) async-start(s32[8,1,48]{2,1,0:T(1,128)} %all_to_all.13), calls=%async_computation.1 | async-start | bytes 8192 | tf_op jit(solution)/shard_map/all_to_all | solution.py:58
  19.9 8.4 %reshape.114 = bf16[256,7168]{1,0:T(8,128)(2,1)} reshape(bf16[128,2,7168]{2,1,0:T(2,128)(2,1)} %param.5) | data formatting | bytes 7340032 | tf_op jit(solution)/shard_map/reshape | solution.py:33
  28.3 10.1 %scatter_custom_fusion = bf16[384,7168]{1,0:T(8,128)(2,1)} fusion(s32[256]{0:T(256)S(1)} %bitcast.28, bf16[256,7168]{1,0:T(8,128)(2,1)} %reshape.114, bf16[]{:T(256)} %constant.13.clone.1), kind=kCustom, calls=%fused_computation.6 | custom fusion | bytes 5505536 | tf_op jit(solution)/shard_map/scatter | solution.py:33
  38.4 4.9 %all-to-all-start = ((bf16[8,48,7168]{2,1,0:T(8,128)(2,1)}), bf16[8,48,7168]{2,1,0:T(8,128)(2,1)}, u32[]{:S(2)}, u32[]{:S(2)}) async-start(bf16[8,48,7168]{2,1,0:T(8,128)(2,1)} %bitcast.24), calls=%async_computation | async-start | bytes 11010048 | tf_op jit(solution)/shard_map/all_to_all | solution.py:44
  43.5 0.1 mul.78
  43.6 1.0 mul.80
  44.7 2.5 mul.81
  47.1 4.5 %scatter_custom_fusion.2 = bf16[384,2048]{1,0:T(8,128)(2,1)} fusion(s32[256]{0:T(256)S(1)} %bitcast.29, f32[256,2048]{1,0:T(8,128)} %mul.81, f32[256]{0:T(256)S(1)} %mul.78, bf16[]{:T(256)} %constant.13.clone.1), kind=kCustom, calls=%fused_computation.14 | custom fusion | flops 1048576 | bytes 3671042 | tf_op jit(solution)/shard_map/scatter | solution.py:38
  51.7 54.6 %all-to-all-done = bf16[8,48,7168]{2,1,0:T(8,128)(2,1)} async-done(((bf16[8,48,7168]{2,1,0:T(8,128)(2,1)}), bf16[8,48,7168]{2,1,0:T(8,128)(2,1)}, u32[]{:S(2)}, u32[]{:S(2)}) %all-to-all-start) | async-done | bytes 5505056 | tf_op jit(solution)/shard_map/all_to_all | solution.py:44
  106.3 4.4 %all-to-all-start.2 = ((bf16[8,48,2048]{2,1,0:T(8,128)(2,1)}), bf16[8,48,2048]{2,1,0:T(8,128)(2,1)S(1)}, u32[]{:S(2)}, u32[]{:S(2)}) async-start(bf16[8,48,2048]{2,1,0:T(8,128)(2,1)} %bitcast.6), calls=%async_computation.2 | async-start | bytes 3145728 | tf_op jit(solution)/shard_map/all_to_all | solution.py:51
  110.6 0.5 broadcast.104
  111.1 0.7 reduce.5
  111.9 8.1 %fusion.15 = f32[384,384]{0,1:T(8,128)S(1)} fusion(bf16[384,7168]{1,0:T(8,128)(2,1)} %bitcast.5), kind=kOutput, calls=%fused_computation.34 | convolution fusion | flops 2113929216 | bytes 6094848 | tf_op jit(solution)/shard_map/dot_general | solution.py:69
  120.0 11.3 %all-to-all-done.2 = bf16[8,48,2048]{2,1,0:T(8,128)(2,1)S(1)} async-done(((bf16[8,48,2048]{2,1,0:T(8,128)(2,1)}), bf16[8,48,2048]{2,1,0:T(8,128)(2,1)S(1)}, u32[]{:S(2)}, u32[]{:S(2)}) %all-to-all-start.2) | async-done | bytes 1572896 | tf_op jit(solution)/shard_map/all_to_all | solution.py:51
  131.4 1.0 fusion.5
  132.4 0.2 fusion.9
  132.6 12.6 %psum.7 = f32[8]{0:T(128)S(1)} all-reduce(f32[8]{0:T(128)S(1)} %fusion.9), channel_id=1, replica_groups=mesh['dp'=16,'expert'=8] {'expert'}, use_global_device_ids=true, to_apply=%region_8.9 | all-reduce | flops 8 | bytes 64 | tf_op jit(solution)/shard_map/psum | solution.py:74
  145.2 0.5 sqrt_multiply_fusion
  145.9 22.0 %bitcast_convert_fusion = bf16[7168,2048]{1,0:T(8,128)(2,1)} fusion(bf16[8,48,7168]{2,1,0:T(8,128)(2,1)} %all-to-all-done, bf16[8,48,2048]{2,1,0:T(8,128)(2,1)S(1)} %all-to-all-done.2, f32[8,48]{1,0:T(8,128)S(1)} %mul.89), kind=kOutput, calls=%fused_computation.3 | convolution fusion | flops 11291328512 | bytes 36439552 | tf_op jit(solution)/shard_map/dot_general | solution.py:81
  167.9 174.1 %reduce-scatter.2.cloned.1.call-done = bf16[448,2048]{1,0:T(8,128)(2,1)} async-done(((bf16[7168,2048]{1,0:T(8,128)(2,1)}), bf16[448,2048]{1,0:T(8,128)(2,1)}) %reduce-scatter.2.cloned.1.call-update) | async-done | bytes 1835024 | tf_op jit(solution)/shard_map/reduce_scatter | solution.py:80
  341.9 3.2 fusion.2
  (18 shorter events, 0.6 us)
Async XLA Ops:
  13.1 25.3 %all-to-all-start.1 = ((s32[8,1,48]{2,1,0:T(1,128)}), s32[8,1,48]{2,1,0:T(1,128)S(1)}, u32[]{:S(2)}, u32[]{:S(2)}) async-start(s32[8,1,48]{2,1,0:T(1,128)} %all_to_all.13), calls=%async_computation.1 | async-start | bytes 8192 | tf_op jit(solution)/shard_map/all_to_all | solution.py:58
  38.4 5.0 %copy-start.1 = (f32[128,2]{0,1:T(2,128)S(1)}, f32[128,2]{0,1:T(2,128)}, u32[]{:S(2)}) copy-start(f32[128,2]{0,1:T(2,128)} %param.7) | copy-start | bytes 3076
  38.4 5.2 %copy-start = (bf16[128,2048]{1,0:T(8,128)(2,1)S(1)}, bf16[128,2048]{1,0:T(8,128)(2,1)}, u32[]{:S(2)}) copy-start(bf16[128,2048]{1,0:T(8,128)(2,1)} %param.6) | copy-start | bytes 1572868
  38.4 67.9 %all-to-all-start = ((bf16[8,48,7168]{2,1,0:T(8,128)(2,1)}), bf16[8,48,7168]{2,1,0:T(8,128)(2,1)}, u32[]{:S(2)}, u32[]{:S(2)}) async-start(bf16[8,48,7168]{2,1,0:T(8,128)(2,1)} %bitcast.24), calls=%async_computation | async-start | bytes 11010048 | tf_op jit(solution)/shard_map/all_to_all | solution.py:44
  106.3 25.1 %all-to-all-start.2 = ((bf16[8,48,2048]{2,1,0:T(8,128)(2,1)}), bf16[8,48,2048]{2,1,0:T(8,128)(2,1)S(1)}, u32[]{:S(2)}, u32[]{:S(2)}) async-start(bf16[8,48,2048]{2,1,0:T(8,128)(2,1)} %bitcast.6), calls=%async_computation.2 | async-start | bytes 3145728 | tf_op jit(solution)/shard_map/all_to_all | solution.py:51
  110.6 231.3 %reduce-scatter.2.cloned.1.call-start = ((), (), s32[]{:S(2)}) async-start(), calls=%async_computation.4 | async-start | bytes 31195136 | tf_op jit(solution)/shard_map/reduce_scatter | solution.py:80
Sparse Core Ops, SparseCore 0:
  168.0 173.8 reduce-scatter.1
where the time goes:
time: 353 us; the launch traced here: 352 us
  waiting for transfers between devices  240 us (68%)
  matrix products  31.1 us (9%)
  local copies, waits for them, and re-layouts  27.4 us (8%)
  starting transfers between devices  16.1 us (5%)
  between operations  14.1 us (4%)
  blocking collectives  12.6 us (4%)
  other arithmetic  10.6 us (3%)
    reduce_scatter x1, waiting for transfers between devices, body(): lax.psum_scatter(lax.dot_general(hidden_in, clipped, (((0,), (0,)), ((),...  174 us
    all_to_all x1, waiting for transfers between devices, body(): lax.all_to_all(hidden_sent.reshape(experts, capacity, hidden_width), 'exp...  54.6 us
    dot_general x1, matrix products, body(): lax.dot_general(hidden_in, clipped, (((0,), (0,)), ((), ())), preferred_e...  22 us
    psum x1, blocking collectives, body(): squares = lax.psum(square_part, 'expert')  12.6 us
    all_to_all x1, waiting for transfers between devices, body(): lax.all_to_all(grads_sent.reshape(experts, capacity, out_width), 'expert'...  11.3 us
    scatter x1, local copies, waits for them, and re-layouts, body(): hidden_sent = jnp.zeros((experts * capacity, hidden_width), jnp.bfloat16)...  10.1 us
    reshape x1, local copies, waits for them, and re-layouts, body(): hidden.reshape(-1, hidden_width)  8.4 us
    dot_general x1, matrix products, body(): jnp.dot(hidden_in, hidden_in.T, preferred_element_type=jnp.float32)  8.14 us
  transfers between devices with their start and end apart: 4, of which 3 were waited for; matrix products, arithmetic and copies ran while one was open for 10% of the time, Pallas kernels for 0%

commit v1 on v0

--- a/solution.py
+++ b/solution.py
@@ -71,7 +71,9 @@
     matched = (owner_in[:, None] == owner_in[None, :]).astype(jnp.float32)
     row_sums = jnp.sum(hidden_gram * grad_gram * matched, axis=1)
     square_part = jnp.sum(row_sums[:, None] * belongs, axis=0)
-    squares = lax.psum(square_part, "expert")
+    squares = square_part
+    for hop in (1, 2, 4):
+        squares = squares + lax.ppermute(squares, "expert", [(dev, dev ^ hop) for dev in range(8)])
     norm_values = jnp.sqrt(squares)
     factors = jnp.minimum(1.0, threshold / norm_values)
     row_factors = jnp.sum(belongs * factors[None, :], axis=1)

time: 353 us -> 350 us (level)
  blocking collectives: 12.6 us -> 0 us
  waiting for transfers between devices: 240 us -> 248 us
    psum x1 -> x0, blocking collectives: 12.6 us -> none  [body(): squares = lax.psum(square_part, 'expert')]
    ppermute x0 -> x3, waiting for transfers between devices: none -> 6.21 us  [body(): lax.ppermute(squares, 'expert', [(dev, dev ^ hop) for dev in range(8)])]
  transfers between devices with their start and end apart: 4 -> 7, of which waited for: 3 -> 6; matrix products, arithmetic and copies ran while one was open for 10% -> 10% of each run, Pallas kernels for 0% -> 0%
where the time goes in v1:
time: 350 us
  waiting for transfers between devices  248 us (71%)
  matrix products  31.1 us (9%)
  local copies, waits for them, and re-layouts  27.4 us (8%)
  starting transfers between devices  18 us (5%)
  between operations  14.1 us (4%)
  other arithmetic  10.6 us (3%)
    reduce_scatter x1, waiting for transfers between devices, body(): lax.psum_scatter(lax.dot_general(hidden_in, clipped, (((0,), (0,)), ((),...  176 us
    all_to_all x1, waiting for transfers between devices, body(): lax.all_to_all(hidden_sent.reshape(experts, capacity, hidden_width), 'exp...  54.6 us
    dot_general x1, matrix products, body(): lax.dot_general(hidden_in, clipped, (((0,), (0,)), ((), ())), preferred_e...  22 us
    all_to_all x1, waiting for transfers between devices, body(): lax.all_to_all(grads_sent.reshape(experts, capacity, out_width), 'expert'...  11.3 us
    scatter x1, local copies, waits for them, and re-layouts, body(): hidden_sent = jnp.zeros((experts * capacity, hidden_width), jnp.bfloat16)...  10.1 us
    reshape x1, local copies, waits for them, and re-layouts, body(): hidden.reshape(-1, hidden_width)  8.4 us
    dot_general x1, matrix products, body(): jnp.dot(hidden_in, hidden_in.T, preferred_element_type=jnp.float32)  8.14 us
  transfers between devices with their start and end apart: 7, of which 6 were waited for; matrix products, arithmetic and copies ran while one was open for 10% of the time, Pallas kernels for 0%

profile of v1, /device:TPU:1, one launch (start us, length us, event | category | flops | bytes accessed | tf_op | source)
XLA Modules:
  0.0 349.6 jit_solution(9516912669223555220)
XLA Ops:
  7.2 0.7 broadcast_multiply_fusion
  7.8 0.8 copy.12
  9.2 0.6 reduce-window.6
  9.8 0.2 slice_reduce_fusion
  10.0 0.7 broadcast_in_dim.10
  11.0 1.4 scatter_custom_fusion.1
  12.4 0.7 all_to_all.13
  13.1 6.8 %all-to-all-start.1 = ((s32[8,1,48]{2,1,0:T(1,128)}), s32[8,1,48]{2,1,0:T(1,128)S(1)}, u32[]{:S(2)}, u32[]{:S(2)}) async-start(s32[8,1,48]{2,1,0:T(1,128)} %all_to_all.13), calls=%async_computation.1 | async-start | bytes 8192 | tf_op jit(solution)/shard_map/all_to_all | solution.py:58
  19.9 8.4 %reshape.114 = bf16[256,7168]{1,0:T(8,128)(2,1)} reshape(bf16[128,2,7168]{2,1,0:T(2,128)(2,1)} %param.5) | data formatting | bytes 7340032 | tf_op jit(solution)/shard_map/reshape | solution.py:33
  28.3 10.1 %scatter_custom_fusion = bf16[384,7168]{1,0:T(8,128)(2,1)} fusion(s32[256]{0:T(256)S(1)} %bitcast.28, bf16[256,7168]{1,0:T(8,128)(2,1)} %reshape.114, bf16[]{:T(256)} %constant.13.clone.1), kind=kCustom, calls=%fused_computation.6 | custom fusion | bytes 5505536 | tf_op jit(solution)/shard_map/scatter | solution.py:33
  38.4 4.9 %all-to-all-start = ((bf16[8,48,7168]{2,1,0:T(8,128)(2,1)}), bf16[8,48,7168]{2,1,0:T(8,128)(2,1)}, u32[]{:S(2)}, u32[]{:S(2)}) async-start(bf16[8,48,7168]{2,1,0:T(8,128)(2,1)} %bitcast.24), calls=%async_computation | async-start | bytes 11010048 | tf_op jit(solution)/shard_map/all_to_all | solution.py:44
  43.6 1.0 mul.80
  44.7 2.5 mul.81
  47.1 4.5 %scatter_custom_fusion.2 = bf16[384,2048]{1,0:T(8,128)(2,1)} fusion(s32[256]{0:T(256)S(1)} %bitcast.29, f32[256,2048]{1,0:T(8,128)} %mul.81, f32[256]{0:T(256)S(1)} %mul.78, bf16[]{:T(256)} %constant.13.clone.1), kind=kCustom, calls=%fused_computation.14 | custom fusion | flops 1048576 | bytes 3671042 | tf_op jit(solution)/shard_map/scatter | solution.py:38
  51.7 54.6 %all-to-all-done = bf16[8,48,7168]{2,1,0:T(8,128)(2,1)} async-done(((bf16[8,48,7168]{2,1,0:T(8,128)(2,1)}), bf16[8,48,7168]{2,1,0:T(8,128)(2,1)}, u32[]{:S(2)}, u32[]{:S(2)}) %all-to-all-start) | async-done | bytes 5505056 | tf_op jit(solution)/shard_map/all_to_all | solution.py:44
  106.3 4.4 %all-to-all-start.2 = ((bf16[8,48,2048]{2,1,0:T(8,128)(2,1)}), bf16[8,48,2048]{2,1,0:T(8,128)(2,1)S(1)}, u32[]{:S(2)}, u32[]{:S(2)}) async-start(bf16[8,48,2048]{2,1,0:T(8,128)(2,1)} %bitcast.6), calls=%async_computation.2 | async-start | bytes 3145728 | tf_op jit(solution)/shard_map/all_to_all | solution.py:51
  110.6 0.5 broadcast.104
  111.1 0.7 reduce.5
  111.9 8.1 %fusion.15 = f32[384,384]{0,1:T(8,128)S(1)} fusion(bf16[384,7168]{1,0:T(8,128)(2,1)} %bitcast.5), kind=kOutput, calls=%fused_computation.35 | convolution fusion | flops 2113929216 | bytes 6094848 | tf_op jit(solution)/shard_map/dot_general | solution.py:69
  120.0 11.3 %all-to-all-done.2 = bf16[8,48,2048]{2,1,0:T(8,128)(2,1)S(1)} async-done(((bf16[8,48,2048]{2,1,0:T(8,128)(2,1)}), bf16[8,48,2048]{2,1,0:T(8,128)(2,1)S(1)}, u32[]{:S(2)}, u32[]{:S(2)}) %all-to-all-start.2) | async-done | bytes 1572896 | tf_op jit(solution)/shard_map/all_to_all | solution.py:51
  131.4 1.0 fusion.5
  132.4 0.2 fusion.9
  132.6 1.0 collective-permute-start
  133.5 0.8 collective-permute-done
  134.3 0.3 collective-permute-start.1
  134.6 2.1 collective-permute-done.1
  136.7 0.6 collective-permute-start.2
  137.3 3.3 collective-permute-done.2
  140.6 0.5 broadcast_multiply_fusion.1
  141.3 22.0 %bitcast_convert_fusion = bf16[7168,2048]{1,0:T(8,128)(2,1)} fusion(bf16[8,48,7168]{2,1,0:T(8,128)(2,1)} %all-to-all-done, bf16[8,48,2048]{2,1,0:T(8,128)(2,1)S(1)} %all-to-all-done.2, f32[8,48]{1,0:T(8,128)S(1)} %mul.89), kind=kOutput, calls=%fused_computation.3 | convolution fusion | flops 11291328512 | bytes 36439552 | tf_op jit(solution)/shard_map/dot_general | solution.py:83
  163.3 176.2 %reduce-scatter.2.cloned.1.call-done = bf16[448,2048]{1,0:T(8,128)(2,1)} async-done(((bf16[7168,2048]{1,0:T(8,128)(2,1)}), bf16[448,2048]{1,0:T(8,128)(2,1)}) %reduce-scatter.2.cloned.1.call-update) | async-done | bytes 1835024 | tf_op jit(solution)/shard_map/reduce_scatter | solution.py:82
  339.5 3.2 fusion.2
  (25 shorter events, 1.4 us)
Async XLA Ops:
  13.1 25.3 %all-to-all-start.1 = ((s32[8,1,48]{2,1,0:T(1,128)}), s32[8,1,48]{2,1,0:T(1,128)S(1)}, u32[]{:S(2)}, u32[]{:S(2)}) async-start(s32[8,1,48]{2,1,0:T(1,128)} %all_to_all.13), calls=%async_computation.1 | async-start | bytes 8192 | tf_op jit(solution)/shard_map/all_to_all | solution.py:58
  38.4 5.0 %copy-start.1 = (f32[128,2]{0,1:T(2,128)S(1)}, f32[128,2]{0,1:T(2,128)}, u32[]{:S(2)}) copy-start(f32[128,2]{0,1:T(2,128)} %param.7) | copy-start | bytes 3076
  38.4 5.2 %copy-start = (bf16[128,2048]{1,0:T(8,128)(2,1)S(1)}, bf16[128,2048]{1,0:T(8,128)(2,1)}, u32[]{:S(2)}) copy-start(bf16[128,2048]{1,0:T(8,128)(2,1)} %param.6) | copy-start | bytes 1572868
  38.4 67.9 %all-to-all-start = ((bf16[8,48,7168]{2,1,0:T(8,128)(2,1)}), bf16[8,48,7168]{2,1,0:T(8,128)(2,1)}, u32[]{:S(2)}, u32[]{:S(2)}) async-start(bf16[8,48,7168]{2,1,0:T(8,128)(2,1)} %bitcast.24), calls=%async_computation | async-start | bytes 11010048 | tf_op jit(solution)/shard_map/all_to_all | solution.py:44
  106.3 25.1 %all-to-all-start.2 = ((bf16[8,48,2048]{2,1,0:T(8,128)(2,1)}), bf16[8,48,2048]{2,1,0:T(8,128)(2,1)S(1)}, u32[]{:S(2)}, u32[]{:S(2)}) async-start(bf16[8,48,2048]{2,1,0:T(8,128)(2,1)} %bitcast.6), calls=%async_computation.2 | async-start | bytes 3145728 | tf_op jit(solution)/shard_map/all_to_all | solution.py:51
  110.6 228.9 %reduce-scatter.2.cloned.1.call-start = ((), (), s32[]{:S(2)}) async-start(), calls=%async_computation.4 | async-start | bytes 31195136 | tf_op jit(solution)/shard_map/reduce_scatter | solution.py:82
  132.6 1.8 collective-permute-start
  134.3 2.4 collective-permute-start.1
  136.7 3.9 %collective-permute-start.2 = (f32[8]{0:T(128)S(1)}, f32[8]{0:T(128)S(1)}, u32[]{:S(2)}, u32[]{:S(2)}) collective-permute-start(f32[8]{0:T(128)S(1)} %add.52), channel_id=1, source_target_pairs={{0,4},{1,5},{2,6},{3,7},{4,0},{5,1},{6,2},{7,3},{8,12},{9,13},{10,... | collective-permute-start | bytes 104 | tf_op jit(solution)/shard_map/ppermute | solution.py:76
Sparse Core Ops, SparseCore 0:
  163.4 176.0 reduce-scatter.1
